TPU v7x, 32 devices: a whole 2x2x4 slice. The times are simulated.
32 devices in a mesh: leaf: 4 (over x, core), oct: 8 (over z, y).
Axes of the slice: x: 2, y: 2, z: 4, core: 2. Of those that a mesh axis runs over, the one named last changes fastest.
Arguments:
- dens_fine: bfloat16 [152, 4608], P(None, ('leaf', 'oct')), may hold values from -6 to 6
- parent: int32 [4608], P(('leaf', 'oct')), may hold values from 0 to 1023, as said below
- child_code: int32 [4608], P(('leaf', 'oct')), may hold values from 0 to 7, as said below
- m2m_ops: bfloat16 [152, 8, 152], replicated, may hold values from -0.15625 to 0.15625
- m2l_ops: bfloat16 [152, 152, 316], replicated, may hold values from -0.02734375 to 0.02734375
- ask_fine: int32 [32, 32, 16], P(('leaf', 'oct')), may hold values from -1 to 143, as said below
- list_fine: int32 [4608, 316], P(('leaf', 'oct')), may hold values from -1 to 655, as said below
- ask_coarse: int32 [32, 32, 8], P(('leaf', 'oct')), may hold values from -1 to 31, as said below
- list_coarse: int32 [1024, 316], P(('leaf', 'oct')), may hold values from -1 to 287, as said below
Outputs:
- pot_fine: float32 [152, 4608], P(None, ('leaf', 'oct'))
- pot_coarse: float32 [152, 1024], P(None, ('leaf', 'oct'))
Inputs may be any that keep to these rules, and one draw needn't show every extreme that they name: parent[i] is a coarse octant of the device that holds fine octant i; parents never fall along the array; every coarse octant has 1 to 8 children and some has 8. `child_code`: the children of one coarse octant carry distinct codes, increasing along the array. ask_fine[d, e] lists distinct fine octants of device e, then -1 to the end; row d, d is all -1; some row holds 16 octants. `list_fine`: an entry other than -1 names an own octant (below 144) or a slot of ask_fine[d] that isn't -1; each target has at most 189 entries other than -1, and some target has exactly 189. ask_coarse[d, e] lists distinct coarse octants of device e, then -1 to the end; row d, d is all -1; some row holds 8 octants. `list_coarse`: an entry other than -1 names an own octant (below 32) or a slot of ask_coarse[d] that isn't -1; each target has at most 189 entries other than -1, and some target has exactly 189.
All inputs are finite; a program needn't handle non-finite values.
Results may differ from a plain program's by a relative error of at most 0.0029.
Values may be sent and summed in bfloat16 or wider, within the bound.
No kernel may reach another device: no remote copies, remote signals or barrier semaphores. Data moves between devices by JAX's collectives and lax.ppermute only.
A program may use at most 192 MiB of HBM per device.

v0:
```python
import functools

import jax
import jax.numpy as jnp
from jax import lax
from jax.experimental import pallas as pl
from jax.experimental.pallas import tpu as pltpu
from jax.sharding import PartitionSpec as P

LANES = 128
CHUNK = 16
HALF = LANES // 2
BLANK = 1 << 20
LOCAL = LANES
AXES = ("leaf", "oct")
STAGE_A, STAGE_B = 23, 3
VMEM_BYTES = 56 << 20


def ceil_to(n, m):
    return (n + m - 1) // m * m


def lane_iota(shape):
    return lax.broadcasted_iota(jnp.int32, shape, 1)


def whole(x):
    return pl.BlockSpec(x.shape, lambda *i: (0,) * x.ndim)


def shape_of(shape, dtype):
    return jax.ShapeDtypeStruct(shape, dtype)


def asks_kernel(fine_own, f_ref, c_ref, o_ref, scr):
    fine_cap, peers = f_ref.shape
    coarse_cap = c_ref.shape[0]
    scr[...] = jnp.zeros_like(scr)
    scr[0:fine_cap, 0:peers] = f_ref[...]
    coarse = c_ref[...]
    scr[fine_cap : fine_cap + coarse_cap, 0:peers] = jnp.where(coarse < 0, -1, coarse + fine_own)
    o_ref[...] = scr[...].T[0:peers, 0 : fine_cap + coarse_cap]


def join_asks(asks_fine, asks_coarse, fine_own):
    peers = asks_fine.shape[1]
    slots = asks_fine.shape[0] + asks_coarse.shape[0]
    return pl.pallas_call(
        functools.partial(asks_kernel, fine_own),
        out_shape=shape_of((peers, slots), jnp.int32),
        scratch_shapes=[pltpu.VMEM((LANES, LANES), jnp.int32)],
        name="join_asks",
    )(asks_fine, asks_coarse)


def answer_kernel(w_ref, f_ref, c_any, o_ref, scr, hot, c_ref, sem):
    peers, slots = w_ref.shape
    own, surface = f_ref.shape[0] + c_ref.shape[0], f_ref.shape[1]
    fetch = pltpu.make_async_copy(c_any, c_ref, sem)
    fetch.start()
    scr[0:peers, 0:slots] = w_ref[...]
    columns = scr[...].T[0:slots, :]
    octant = lane_iota((slots, own))
    for e in range(0, peers, 2):
        picked = [
            jnp.broadcast_to(columns[:, d : d + 1], (slots, own)) == octant for d in (e, e + 1)
        ]
        both = jnp.concatenate([p.astype(jnp.float32) for p in picked], axis=0)
        hot[e * slots : (e + 2) * slots, :] = both.astype(jnp.bfloat16)
    fetch.wait()
    rows = jnp.concatenate([f_ref[...], c_ref[...]], axis=0)
    found = jnp.dot(hot[...], rows, preferred_element_type=jnp.float32)
    extra = surface - LANES
    rest = jnp.concatenate(
        [found[:, LANES:], jnp.zeros((peers * slots, LANES - extra), jnp.float32)], axis=1
    ).reshape(peers, slots, LANES)
    line = rest[:, 0:8].reshape(peers * 8, LANES)
    for g in range(1, slots // 8):
        part = rest[:, 8 * g : 8 * g + 8].reshape(peers * 8, LANES)
        line = line + pltpu.roll(part, g * extra, axis=1)
    o_ref[...] = jnp.concatenate(
        [found[:, 0:LANES].reshape(peers, slots, LANES), line.reshape(peers, 8, LANES)], axis=1
    ).astype(jnp.bfloat16)


def answer(wanted, fine_rows, coarse_rows):
    peers, slots = wanted.shape
    own = fine_rows.shape[0] + coarse_rows.shape[0]
    return pl.pallas_call(
        answer_kernel,
        in_specs=[whole(wanted), whole(fine_rows), pl.BlockSpec(memory_space=pl.ANY)],
        out_shape=shape_of((peers, slots + 8, LANES), jnp.bfloat16),
        scratch_shapes=[
            pltpu.VMEM((LANES, LANES), jnp.int32),
            pltpu.VMEM((peers * slots, own), jnp.bfloat16),
            pltpu.VMEM(coarse_rows.shape, jnp.bfloat16),
            pltpu.SemaphoreType.DMA,
        ],
        name="answer",
    )(wanted, fine_rows, coarse_rows)


def remap(entries, own, done, cap, shift):
    slot = jnp.maximum(entries - own, 0)
    peer = slot // cap
    moved = jnp.take_along_axis(
        jnp.broadcast_to(shift, entries.shape), peer, axis=1, mode="promise_in_bounds"
    )
    column = jnp.where(entries < own, entries, entries - moved) - done
    return jnp.where(entries < done, BLANK, column)


def plan_kernel(
    variants,
    coarse_at,
    af_ref,
    ac_ref,
    lf_ref,
    lc_ref,
    idx_ref,
    tail_ref,
    to_ref,
    pick_ref,
    own_idx_ref,
    own_tail_ref,
    cnt,
):
    offsets = lf_ref.shape[1]
    body_lanes = idx_ref.shape[1]
    peers = af_ref.shape[1]
    lanes = lane_iota((LANES, LANES))
    earlier = lax.broadcasted_iota(jnp.int32, (LANES, LANES), 0) < lanes
    earlier = earlier.astype(jnp.float32).astype(jnp.bfloat16)
    levels = []
    row = tail_row = 0
    cnt[...] = jnp.zeros_like(cnt)
    for level, (ask_ref, list_ref) in enumerate(((af_ref, lf_ref), (ac_ref, lc_ref))):
        own, cap = list_ref.shape[0], ask_ref.shape[0]
        done = LOCAL if level == 0 else 0
        valid = (ask_ref[...] >= 0).astype(jnp.float32)
        cnt[level, 0:1, 0:peers] = jnp.sum(valid, axis=0, keepdims=True)
        counts = cnt[level]
        before = jnp.dot(
            counts.astype(jnp.bfloat16), earlier, preferred_element_type=jnp.float32
        ).astype(jnp.int32)[0:1]
        total = jnp.sum(counts).astype(jnp.int32)
        counts = counts.astype(jnp.int32)[0:1]
        shift = lane_iota((1, LANES)) * cap - before
        levels.append((own, cap, counts, before, total))
        lists = [list_ref[:, first : first + LANES] for first in range(0, body_lanes, LANES)]
        lists.append(
            jnp.concatenate(
                [
                    list_ref[:, body_lanes:offsets],
                    jnp.full((own, LANES - (offsets - body_lanes)), -1, jnp.int32),
                ],
                axis=1,
            )
        )
        upper = tail_rows(own)

        def keep(columns, to_body, to_tail, at, tail_at):
            for k, x in enumerate(columns[:-1]):
                to_body[at : at + own, k * LANES : (k + 1) * LANES] = x
            rest = columns[-1]
            moved = pltpu.roll(rest[upper:], HALF, axis=1)
            if own - upper < upper:
                missing = jnp.full((2 * upper - own, LANES), BLANK, jnp.int32)
                moved = jnp.concatenate([moved, missing], axis=0)
            to_tail[tail_at : tail_at + upper, :] = jnp.where(
                lane_iota((upper, LANES)) < HALF, rest[0:upper], moved
            )

        keep([remap(x, own, done, cap, shift) for x in lists], idx_ref, tail_ref, row, tail_row)
        if level == 0:
            near = [jnp.where((x < 0) | (x >= LOCAL), BLANK, x) for x in lists]
            keep(near, own_idx_ref, own_tail_ref, 0, 0)
        row += own
        tail_row += upper

    (fine_own, fine_cap, *fine), (coarse_own, coarse_cap, *coarse) = levels
    place = lax.broadcasted_iota(jnp.int32, (8, LANES), 0)
    at = 0
    for level, base in (((fine_cap, *fine), fine_own - LOCAL), ((coarse_cap, *coarse), coarse_at + coarse_own)):
        cap, counts, before, _ = level
        for first in range(0, cap, 8):
            for e in range(peers):
                count = jnp.broadcast_to(counts[:, e : e + 1], (8, LANES))
                start = jnp.broadcast_to(before[:, e : e + 1], (8, LANES)) + base
                k = place + first
                to_ref[at : at + 8, :] = jnp.where(k < count, start + k, -1)
                at += 8
    octant = lax.broadcasted_iota(jnp.int32, (fine_own, LANES), 0)
    to_ref[at : at + fine_own, :] = jnp.maximum(octant - LOCAL, -1)
    octant = lax.broadcasted_iota(jnp.int32, (coarse_own, LANES), 0)
    to_ref[at + fine_own : at + row, :] = octant + coarse_at

    pick = jnp.int32(len(variants) - 1)
    for at in reversed(range(len(variants) - 1)):
        fits = (fine_own - LOCAL + fine[2] <= variants[at][0] * LANES) & (
            coarse_own + coarse[2] <= variants[at][1] * LANES
        )
        pick = jnp.where(fits, at, pick)
    pick_ref[0] = pick


def plan(asks_fine, asks_coarse, list_fine, list_coarse, variants, coarse_at):
    own = list_fine.shape[0] + list_coarse.shape[0]
    tails = sum(tail_rows(x.shape[0]) for x in (list_fine, list_coarse))
    body_lanes = list_fine.shape[1] // LANES * LANES
    slots, peers = asks_fine.shape[0] + asks_coarse.shape[0], asks_fine.shape[1]
    vmem = pl.BlockSpec(memory_space=pltpu.VMEM)
    return pl.pallas_call(
        functools.partial(plan_kernel, variants, coarse_at),
        out_specs=[vmem, vmem, vmem, pl.BlockSpec(memory_space=pltpu.SMEM), vmem, vmem],
        out_shape=[
            shape_of((own, body_lanes), jnp.int32),
            shape_of((tails, LANES), jnp.int32),
            shape_of((own + peers * slots, LANES), jnp.int32),
            shape_of((1,), jnp.int32),
            shape_of((list_fine.shape[0], body_lanes), jnp.int32),
            shape_of((tail_rows(list_fine.shape[0]), LANES), jnp.int32),
        ],
        scratch_shapes=[pltpu.VMEM((2, 8, LANES), jnp.float32)],
        compiler_params=pltpu.CompilerParams(vmem_limit_bytes=VMEM_BYTES),
        name="plan",
    )(asks_fine, asks_coarse, list_fine, list_coarse)


def pack_rows(values, table, tile):
    pairs = values.shape[0] // 2
    even = values[pl.ds(0, pairs, stride=2), :].astype(jnp.int32)
    odd = values[pl.ds(1, pairs, stride=2), :].astype(jnp.int32)
    both = odd * 65536 + even
    for block in range(pairs // 4):
        table[block, 0:4, tile * LANES : (tile + 1) * LANES] = both[4 * block : 4 * block + 4]


def scale_of(values):
    peak = jnp.max(jnp.max(jnp.abs(values), axis=0, keepdims=True), axis=1, keepdims=True)
    power = jnp.floor(jnp.log2(jnp.broadcast_to(jnp.maximum(peak, 1e-30), (8, LANES))))
    return jnp.exp2(13.0 - power)[0:1], jnp.exp2(power - 29.0)


def build_tables(ranges, to_ref, f_ref, c_ref, arrived, rows_t, table_f, table, unit):
    peers, lines, _ = arrived.shape
    surface = rows_t.shape[0]
    extra = surface - LANES
    came = arrived[...].astype(jnp.float32)
    rest = came[:, lines - 8 :].reshape(peers * 8, LANES).T
    at = 0
    for g in range(lines // 8 - 1):
        part = came[:, 8 * g : 8 * g + 8].reshape(peers * 8, LANES).T
        part = jnp.concatenate([part, rest[g * extra : (g + 1) * extra]], axis=0)
        rows_t[:, at : at + peers * 8] = part.astype(jnp.bfloat16)
        at += peers * 8
    own = jnp.concatenate([f_ref[...], c_ref[...]], axis=0).astype(jnp.float32)
    rows_t[:, at : at + own.shape[0]] = own.T.astype(jnp.bfloat16)
    to = to_ref[...]
    tiles = table_f.shape[0]
    lanes = lane_iota(to.shape)
    for k in range(0, tiles, 2):
        size = min(2, tiles - k)
        hot = [(to == lanes + (k + h) * LANES).astype(jnp.float32) for h in range(size)]
        hot = jnp.concatenate([x.astype(jnp.bfloat16) for x in hot], axis=1)
        columns = jnp.dot(rows_t[...], hot, preferred_element_type=jnp.float32)
        for h in range(size):
            table_f[k + h] = columns[:, h * LANES : (h + 1) * LANES]
    for level, (low, high) in enumerate(ranges):
        factor, unit[level] = scale_of(jnp.max(jnp.abs(table_f[low:high]), axis=0))
        for k in range(low, high):
            table_f[k] = jnp.round(table_f[k] * factor)
            pack_rows(table_f.at[k], table, k)


def stage_block(m_ref, stage):
    surface, _, offsets = m_ref.shape
    for tile, first in enumerate(range(0, offsets, LANES)):
        size = min(LANES, offsets - first)
        for a in range(surface):
            part = m_ref[a, :, first : first + size].astype(jnp.float32)
            if size < LANES:
                gap = jnp.zeros((8, HALF - size), jnp.float32)
                part = jnp.concatenate([part, gap, part, gap], axis=1)
            stage[tile, pl.ds(STAGE_A * a, 8, stride=STAGE_B), :] = part


def lay_half(half, stage, *mr_refs):
    surface = mr_refs[0].shape[0]
    tiles = stage.shape[0]
    for j in range(4):
        for tile in range(tiles):
            rows = stage[tile, pl.ds(STAGE_B * (4 * half + j), surface, stride=STAGE_A), :]
            at = (j * tiles + tile) * LANES
            for mr_ref in mr_refs:
                mr_ref[:, at : at + LANES] = rows.astype(jnp.bfloat16)


def gather_half(half, step, levels, idx_ref, tail_ref, table, g_ref):
    body_lanes = idx_ref.shape[1]
    width = body_lanes + LANES
    lower = lane_iota((CHUNK, LANES)) < HALF

    def put(rows, q, at, value):
        to = 2 * q * width + at
        low = (value << 16).astype(jnp.float32).astype(jnp.bfloat16)
        high = value.astype(jnp.float32).astype(jnp.bfloat16)
        g_ref[rows : rows + CHUNK, to : to + LANES] = low
        g_ref[rows : rows + CHUNK, to + width : to + width + LANES] = high

    for low, high, base, tiles, tail_row in levels:
        rows = [
            [
                jnp.broadcast_to(
                    table[step, pair : pair + 1, (base + k) * LANES : (base + k + 1) * LANES],
                    (CHUNK, LANES),
                )
                for k in range(tiles)
            ]
            for pair in (2 * half, 2 * half + 1)
        ]

        def gathered(idx):
            at = idx & (LANES - 1)
            later = [idx >= k * LANES for k in range(1, tiles)]
            blank = idx >= BLANK
            for q in range(2):
                value = None
                for k in range(tiles):
                    got = jnp.take_along_axis(rows[q][k], at, axis=1, mode="promise_in_bounds")
                    value = got if k == 0 else jnp.where(later[k - 1], got, value)
                yield q, jnp.where(blank, 0, value)

        for first in range(0, body_lanes, LANES):
            for target in range(low, high, CHUNK):
                idx = idx_ref[target : target + CHUNK, first : first + LANES]
                for q, value in gathered(idx):
                    put(target, q, first, value)
        upper = tail_rows(high - low)
        for target in range(low, low + upper, CHUNK):
            at = tail_row + target - low
            for q, value in gathered(tail_ref[at : at + CHUNK, :]):
                put(target, q, body_lanes, jnp.where(lower, value, 0))
                if target + upper < high:
                    put(target + upper, q, body_lanes, jnp.where(lower, 0, value))


def multiply(acc, g_ref, mr):
    acc[...] += lax.dot_general(
        g_ref[...], mr, (((1,), (1,)), ((), ())), preferred_element_type=jnp.float32
    )


def tail_rows(own):
    return ceil_to(own // CHUNK, 2) // 2 * CHUNK


def local_kernel(
    f_ref, idx_ref, tail_ref, m_ref, _, mr_ref, o_ref, table_f, table, unit, stage, acc, mr_b, g_a, g_b
):
    own = f_ref.shape[0]
    half = mr_ref.shape[1] // 2
    step = pl.program_id(0)

    @pl.when(step == 0)
    def _():
        table_f[...] = f_ref[0:LOCAL, :].astype(jnp.float32).T
        factor, unit[...] = scale_of(table_f[...])
        table_f[...] = jnp.round(table_f[...] * factor)
        pack_rows(table_f, table, 0)
        acc[...] = jnp.zeros_like(acc)
        mr_b[...] = jnp.zeros_like(mr_b)
        g_b[...] = jnp.zeros_like(g_b)

    levels = ((0, own, 0, 1, 0),)
    stage_block(m_ref, stage)
    lay_half(0, stage, mr_ref.at[:, 0:half])
    multiply(acc, g_b, mr_b[...])
    gather_half(0, step, levels, idx_ref, tail_ref, table, g_a)
    lay_half(1, stage, mr_ref.at[:, half : 2 * half], mr_b)
    multiply(acc, g_a, mr_ref[:, 0:half])
    gather_half(1, step, levels, idx_ref, tail_ref, table, g_b)

    @pl.when(step == pl.num_programs(0) - 1)
    def _():
        multiply(acc, g_b, mr_b[...])
        o_ref[...] = acc[...] * unit[0:1, 0:1]


def local_part(fine_rows, idx, tail, m2l_ops, after):
    surface, _, offsets = m2l_ops.shape
    width = ceil_to(offsets, LANES)
    own = fine_rows.shape[0]
    blocks = surface // 8
    return pl.pallas_call(
        local_kernel,
        grid=(blocks,),
        in_specs=[
            whole(fine_rows),
            whole(idx),
            whole(tail),
            pl.BlockSpec((surface, 8, offsets), lambda i: (0, i, 0)),
            pl.BlockSpec(memory_space=pl.ANY),
        ],
        out_specs=[
            pl.BlockSpec((None, surface, 8 * width), lambda i: (i, 0, 0)),
            pl.BlockSpec((own, surface), lambda i: (0, 0)),
        ],
        out_shape=[
            shape_of((blocks, surface, 8 * width), jnp.bfloat16),
            shape_of((own, surface), jnp.float32),
        ],
        scratch_shapes=[
            pltpu.VMEM((surface, LANES), jnp.float32),
            pltpu.VMEM((blocks, 8, LANES), jnp.int32),
            pltpu.VMEM((8, LANES), jnp.float32),
            pltpu.VMEM((width // LANES, ceil_to(STAGE_A * surface, 8), LANES), jnp.float32),
            pltpu.VMEM((own, surface), jnp.float32),
            pltpu.VMEM((surface, 4 * width), jnp.bfloat16),
            pltpu.VMEM((own, 4 * width), jnp.bfloat16),
            pltpu.VMEM((own, 4 * width), jnp.bfloat16),
        ],
        compiler_params=pltpu.CompilerParams(vmem_limit_bytes=VMEM_BYTES),
        cost_estimate=pl.CostEstimate(
            flops=2 * surface * surface * own * width,
            bytes_accessed=4 * surface * surface * width,
            transcendentals=0,
        ),
        name="local_part",
    )(fine_rows, idx, tail, m2l_ops, after)


def translate_kernel(
    variants,
    coarse_tile,
    pick_ref,
    idx_ref,
    tail_ref,
    to_ref,
    f_ref,
    c_ref,
    arrived_any,
    part_ref,
    ma_ref,
    mb_ref,
    of_ref,
    oc_ref,
    rows_t,
    table_f,
    table,
    unit,
    arrived,
    acc,
    g_a,
    g_b,
    sem,
):
    fine_own, targets = of_ref.shape[0], idx_ref.shape[0]
    step = pl.program_id(0)
    last = pl.num_programs(0) - 1

    @pl.when(step == 0)
    def _():
        fetch = pltpu.make_async_copy(arrived_any, arrived, sem)
        fetch.start()
        acc[...] = jnp.zeros_like(acc)
        g_b[...] = jnp.zeros_like(g_b)
        fetch.wait()
        build_tables(
            ((0, coarse_tile), (coarse_tile, table_f.shape[0])),
            to_ref,
            f_ref,
            c_ref,
            arrived,
            rows_t,
            table_f,
            table,
            unit,
        )

    def work(fine_tiles, coarse_tiles):
        levels = (
            (0, fine_own, 0, fine_tiles, 0),
            (fine_own, targets, coarse_tile, coarse_tiles, tail_rows(fine_own)),
        )
        multiply(acc, g_b, mb_ref[...])
        gather_half(0, step, levels, idx_ref, tail_ref, table, g_a)
        multiply(acc, g_a, ma_ref[...])
        gather_half(1, step, levels, idx_ref, tail_ref, table, g_b)

    for at, tiles in enumerate(variants):
        pl.when((pick_ref[0] == at) & (step < last))(functools.partial(work, *tiles))

    @pl.when(step == last)
    def _():
        multiply(acc, g_b, mb_ref[...])
        of_ref[...] = acc[0:fine_own, :] * unit[0, 0:1, 0:1] + part_ref[...]
        oc_ref[...] = acc[fine_own:targets, :] * (0.5 * unit[1, 0:1, 0:1])


def translate(
    pick, idx, tail, to, fine_rows, coarse_rows, arrived, part, operators, variants, coarse_tile, tiles
):
    blocks, surface, depth = operators.shape
    targets = idx.shape[0]
    fine_own, coarse_own = fine_rows.shape[0], coarse_rows.shape[0]
    return pl.pallas_call(
        functools.partial(translate_kernel, variants, coarse_tile),
        grid=(blocks + 1,),
        in_specs=[
            pl.BlockSpec(memory_space=pltpu.SMEM),
            whole(idx),
            whole(tail),
            whole(to),
            whole(fine_rows),
            whole(coarse_rows),
            pl.BlockSpec(memory_space=pl.ANY),
            whole(part),
            pl.BlockSpec((None, surface, depth // 2), lambda i: (jnp.minimum(i, blocks - 1), 0, 0)),
            pl.BlockSpec((None, surface, depth // 2), lambda i: (jnp.maximum(i - 1, 0), 0, 1)),
        ],
        out_specs=[
            pl.BlockSpec((fine_own, surface), lambda i: (0, 0)),
            pl.BlockSpec((coarse_own, surface), lambda i: (0, 0)),
        ],
        out_shape=[
            shape_of((fine_own, surface), jnp.float32),
            shape_of((coarse_own, surface), jnp.float32),
        ],
        scratch_shapes=[
            pltpu.VMEM((surface, to.shape[0]), jnp.bfloat16),
            pltpu.VMEM((tiles, surface, LANES), jnp.float32),
            pltpu.VMEM((blocks, 8, tiles * LANES), jnp.int32),
            pltpu.VMEM((2, 8, LANES), jnp.float32),
            pltpu.VMEM(arrived.shape, jnp.bfloat16),
            pltpu.VMEM((targets, surface), jnp.float32),
            pltpu.VMEM((targets, depth // 2), jnp.bfloat16),
            pltpu.VMEM((targets, depth // 2), jnp.bfloat16),
            pltpu.SemaphoreType.DMA,
        ],
        compiler_params=pltpu.CompilerParams(vmem_limit_bytes=VMEM_BYTES),
        cost_estimate=pl.CostEstimate(
            flops=blocks * surface * targets * depth * 2,
            bytes_accessed=2 * blocks * surface * depth,
            transcendentals=0,
        ),
        name="translate",
    )(pick, idx, tail, to, fine_rows, coarse_rows, arrived, part, operators, operators)


def exchange(x):
    return lax.all_to_all(x, AXES, split_axis=0, concat_axis=0, tiled=True)


def body(
    dens_fine, parent, child_code, m2m_ops, m2l_ops, ask_fine, list_fine, ask_coarse, list_coarse
):
    surface, fine_own = dens_fine.shape
    coarse_own = list_coarse.shape[0]
    asks_fine, asks_coarse = ask_fine[0].T, ask_coarse[0].T
    fine_cap, peers = asks_fine.shape
    coarse_cap = asks_coarse.shape[0]
    wanted = exchange(join_asks(asks_fine, asks_coarse, fine_own))

    fine_tiles = ceil_to(fine_own - LOCAL + (peers - 1) * fine_cap, LANES) // LANES
    coarse_tiles = ceil_to(coarse_own + (peers - 1) * coarse_cap, LANES) // LANES
    variants = [(min(n, fine_tiles), min(2, coarse_tiles)) for n in (2, 3)]
    variants = variants + [(fine_tiles, coarse_tiles)]
    idx, tail, to, pick, own_idx, own_tail = plan(
        asks_fine, asks_coarse, list_fine, list_coarse, variants, fine_tiles * LANES
    )

    fine_rows = dens_fine.T
    positions = jnp.arange(8, dtype=jnp.int32)
    spread = jnp.where(
        (child_code[:, None] == positions[None, :])[:, :, None],
        fine_rows[:, None, :],
        jnp.zeros((), jnp.bfloat16),
    )
    child_terms = lax.dot_general(
        spread.reshape(fine_own, 8 * surface),
        m2m_ops.reshape(surface, 8 * surface),
        (((1,), (1,)), ((), ())),
        preferred_element_type=jnp.float32,
    )
    local_parent = parent - lax.axis_index(AXES) * coarse_own
    members = (jnp.arange(coarse_own, dtype=jnp.int32)[:, None] == local_parent[None, :]).astype(
        jnp.float32
    )
    coarse_rows = jnp.dot(members, child_terms, precision=lax.Precision.HIGHEST).astype(
        jnp.bfloat16
    )

    arrived = exchange(answer(wanted, fine_rows, coarse_rows))
    operators, part = local_part(fine_rows, own_idx, own_tail, m2l_ops, wanted)
    pot_fine, pot_coarse = translate(
        pick,
        idx,
        tail,
        to,
        fine_rows,
        coarse_rows,
        arrived,
        part,
        operators,
        variants,
        fine_tiles,
        fine_tiles + coarse_tiles,
    )
    return pot_fine.T, pot_coarse.T


def solution(mesh):
    return jax.shard_map(
        body,
        mesh=mesh,
        in_specs=(
            P(None, AXES),
            P(AXES),
            P(AXES),
            P(),
            P(),
            P(AXES, None, None),
            P(AXES, None),
            P(AXES, None, None),
            P(AXES, None),
        ),
        out_specs=(P(None, AXES), P(None, AXES)),
        check_vma=False,
    )
```

profile of v0, /device:TPU:13, one launch (start us, length us, event | category | flops | bytes accessed | tf_op | source)
XLA Modules:
  0.0 85.6 jit_solution(8526080794323192279)
XLA Ops:
  0.6 0.0 copy-start
  0.6 1.5 %join_asks.1 = s32[32,24]{1,0:T(8,128)} custom-call(s32[16,32]{1,0:T(8,128)} %bitcast.23, s32[8,32]{1,0:T(8,128)} %bitcast.25), custom_call_target="tpu_custom_call" | custom-call | tf_op jit(solution)/shard_map/join_asks/pallas_call | solution.py:49
  2.1 6.3 %all-to-all-start = ((s32[32,1,24]{2,1,0:T(1,128)}), s32[32,1,24]{2,1,0:T(1,128)S(1)}, u32[]{:S(2)}, u32[]{:S(2)}) async-start(s32[32,1,24]{2,1,0:T(1,128)} %bitcast.22), calls=%async_computation | async-start | bytes 32768 | tf_op jit(solution)/shard_map/all_to_all | solution.py:553
  8.4 0.8 iota_compare_fusion
  9.2 0.7 broadcast_subtract_fusion
  9.9 1.1 %broadcast_select_fusion = bf16[144,8,152]{2,1,0:T(8,128)(2,1)S(1)} fusion(pred[144,8]{1,0:T(8,128)(4,1)S(1)} %iota_compare_fusion, bf16[144,152]{1,0:T(8,128)(2,1)} %bitcast.16), kind=kLoop, calls=%fused_computation.4 | loop fusion | flops 175104 | bytes 395136 | tf_op jit(solution)/shard_map/jit(_where)/select_n | solution.py:576
  11.0 0.0 copy-done
  11.0 0.4 convolution_bitcast_fusion
  11.4 0.8 convolution_convert_fusion.c_any.c_ref
  12.2 0.9 %all-to-all-done = s32[32,1,24]{2,1,0:T(1,128)S(1)} async-done(((s32[32,1,24]{2,1,0:T(1,128)}), s32[32,1,24]{2,1,0:T(1,128)S(1)}, u32[]{:S(2)}, u32[]{:S(2)}) %all-to-all-start) | async-done | bytes 3104 | tf_op jit(solution)/shard_map/all_to_all | solution.py:553
  13.1 0.0 copy-start.2
  13.1 0.6 copy-done.2
  13.7 2.7 %answer.1 = bf16[32,32,128]{2,1,0:T(8,128)(2,1)} custom-call(s32[32,24]{1,0:T(8,128)} %bitcast.20, bf16[144,152]{1,0:T(8,128)(2,1)} %bitcast.17, bf16[32,152]{1,0:T(8,128)(2,1)} %convolution_convert_fusion.c_any.c_ref), custom_call_target="tpu_custom_call" | custom-call | tf_op jit(solution)/shard_map/answer/pallas_call | solution.py:90
  16.3 5.0 %all-to-all-start.1 = ((bf16[32,32,128]{2,1,0:T(8,128)(2,1)}), bf16[32,32,128]{2,1,0:T(8,128)(2,1)S(1)}, u32[]{:S(2)}, u32[]{:S(2)}) async-start(bf16[32,32,128]{2,1,0:T(8,128)(2,1)} %answer.1), calls=%async_computation.1 | async-start | bytes 524288 | tf_op jit(solution)/shard_map/all_to_all | solution.py:553
  21.3 2.5 %plan.1 = (s32[176,256]{1,0:T(8,128)}, s32[96,128]{1,0:T(8,128)}, s32[944,128]{1,0:T(8,128)}, s32[1]{0:T(128)}, s32[144,256]{1,0:T(8,128)}, /*index=5*/s32[80,128]{1,0:T(8,128)}) custom-call(s32[16,32]{1,0:T(8,128)} %bitcast.24, s32[8,32]{1,0:T(8,128)} %bitcast.26, s32[144,316]{1,0:T(8,128)} %lf_ref.1, s32[32,316]{1,0:T(8,128)} %lc_ref.1), custom_call_target="tpu_custom_call" | custom-call | tf_op jit(solution)/shard_map/plan/pallas_call | solution.py:214
  23.8 26.5 %local_part.1 = (bf16[19,152,3072]{2,1,0:T(8,128)(2,1)}, f32[144,152]{1,0:T(8,128)}) custom-call(bf16[144,152]{1,0:T(8,128)(2,1)} %bitcast.18, s32[144,256]{1,0:T(8,128)} %get-tuple-element.16.idx_ref, s32[80,128]{1,0:T(8,128)} %get-tuple-element.17.tail_ref, bf16[152,152,316]{2,1,0:T(8,128)(2,1)} %m_ref.1, s32[32,24]{1,0:T(8,128)} %bitcast.21), custom_call_target="tpu_custom_call" | custom-call | flops 2555117568 | bytes 35487744 | tf_op jit(solution)/shard_map/local_part/pallas_call | solution.py:396
  50.3 0.0 all-to-all-done.1.arrived_any
  50.3 0.0 copy-start.1
  50.3 0.7 copy-done.1
  51.0 34.6 %translate.1 = (f32[144,152]{1,0:T(8,128)}, f32[32,152]{1,0:T(8,128)}) custom-call(s32[1]{0:T(128)} %get-tuple-element.12.pick_ref, s32[176,256]{1,0:T(8,128)} %get-tuple-element.13.idx_ref, s32[96,128]{1,0:T(8,128)} %get-tuple-element.14.tail_ref, s32[944,128]{1,0:T(8,128)} %get-tuple-element.15.to_ref, bf16[144,152]{1,0:T(8,128)(2,1)} %bitcast.19, ...), custom_call_target="tpu_custom_call" | custom-call | flops 3122921472 | bytes 17743872 | tf_op jit(solution)/shard_map/translate/pallas_call | solution.py:508
Async XLA Ops:
  0.6 10.4 %copy-start = (bf16[152,8,152]{2,1,0:T(8,128)(2,1)S(1)}, bf16[152,8,152]{2,1,0:T(8,128)(2,1)}, u32[]{:S(2)}) copy-start(bf16[152,8,152]{2,1,0:T(8,128)(2,1)} %param.12) | copy-start | bytes 1108996
  2.1 11.0 %all-to-all-start = ((s32[32,1,24]{2,1,0:T(1,128)}), s32[32,1,24]{2,1,0:T(1,128)S(1)}, u32[]{:S(2)}, u32[]{:S(2)}) async-start(s32[32,1,24]{2,1,0:T(1,128)} %bitcast.22), calls=%async_computation | async-start | bytes 32768 | tf_op jit(solution)/shard_map/all_to_all | solution.py:553
  13.1 0.6 copy-start.2
  16.3 33.9 %all-to-all-start.1 = ((bf16[32,32,128]{2,1,0:T(8,128)(2,1)}), bf16[32,32,128]{2,1,0:T(8,128)(2,1)S(1)}, u32[]{:S(2)}, u32[]{:S(2)}) async-start(bf16[32,32,128]{2,1,0:T(8,128)(2,1)} %answer.1), calls=%async_computation.1 | async-start | bytes 524288 | tf_op jit(solution)/shard_map/all_to_all | solution.py:553
  50.3 0.7 copy-start.1
where the time goes:
time: 86.9 us; the launch traced here: 85.6 us
  Pallas kernels  67.6 us (78%)
  starting transfers between devices  11.3 us (13%)
  other arithmetic  2.55 us (3%)
  local copies, waits for them, and re-layouts  1.3 us (1%)
  matrix products  1.2 us (1%)
    pallas_call x1, Pallas kernels, translate(): pl.pallas_call(functools.partial(translate_kernel, variants, coarse_tile)...  34.6 us
    pallas_call x1, Pallas kernels, local_part(): pl.pallas_call(local_kernel, grid=(blocks,), in_specs=[whole(fine_rows),...  26.5 us
    all_to_all x2, starting transfers between devices, exchange(): return lax.all_to_all(x, AXES, split_axis=0, concat_axis=0, tiled=True)  11.3 us
    pallas_call x1, Pallas kernels, answer(): pl.pallas_call(answer_kernel, in_specs=[whole(wanted), whole(fine_rows),...  2.65 us
    pallas_call x1, Pallas kernels, plan(): pl.pallas_call(functools.partial(plan_kernel, variants, coarse_at), out_s...  2.47 us
  transfers between devices with their start and end apart: 2, of which 1 were waited for; matrix products, arithmetic and copies ran while one was open for 4% of the time, Pallas kernels for 34%

commit v1 on v0

--- a/solution.py
+++ b/solution.py
@@ -11,7 +11,7 @@
 CHUNK = 16
 HALF = LANES // 2
 BLANK = 1 << 20
-LOCAL = LANES
+LOCAL = 0
 AXES = ("leaf", "oct")
 STAGE_A, STAGE_B = 23, 3
 VMEM_BYTES = 56 << 20
@@ -122,8 +122,6 @@
     tail_ref,
     to_ref,
     pick_ref,
-    own_idx_ref,
-    own_tail_ref,
     cnt,
 ):
     offsets = lf_ref.shape[1]
@@ -173,9 +171,6 @@
             )
 
         keep([remap(x, own, done, cap, shift) for x in lists], idx_ref, tail_ref, row, tail_row)
-        if level == 0:
-            near = [jnp.where((x < 0) | (x >= LOCAL), BLANK, x) for x in lists]
-            keep(near, own_idx_ref, own_tail_ref, 0, 0)
         row += own
         tail_row += upper
 
@@ -213,14 +208,12 @@
     vmem = pl.BlockSpec(memory_space=pltpu.VMEM)
     return pl.pallas_call(
         functools.partial(plan_kernel, variants, coarse_at),
-        out_specs=[vmem, vmem, vmem, pl.BlockSpec(memory_space=pltpu.SMEM), vmem, vmem],
+        out_specs=[vmem, vmem, vmem, pl.BlockSpec(memory_space=pltpu.SMEM)],
         out_shape=[
             shape_of((own, body_lanes), jnp.int32),
             shape_of((tails, LANES), jnp.int32),
             shape_of((own + peers * slots, LANES), jnp.int32),
             shape_of((1,), jnp.int32),
-            shape_of((list_fine.shape[0], body_lanes), jnp.int32),
-            shape_of((tail_rows(list_fine.shape[0]), LANES), jnp.int32),
         ],
         scratch_shapes=[pltpu.VMEM((2, 8, LANES), jnp.float32)],
         compiler_params=pltpu.CompilerParams(vmem_limit_bytes=VMEM_BYTES),
@@ -280,21 +273,17 @@
         size = min(LANES, offsets - first)
         for a in range(surface):
             part = m_ref[a, :, first : first + size].astype(jnp.float32)
-            if size < LANES:
-                gap = jnp.zeros((8, HALF - size), jnp.float32)
-                part = jnp.concatenate([part, gap, part, gap], axis=1)
-            stage[tile, pl.ds(STAGE_A * a, 8, stride=STAGE_B), :] = part
-
-
-def lay_half(half, stage, *mr_refs):
-    surface = mr_refs[0].shape[0]
+            stage[tile, pl.ds(STAGE_A * a, 8, stride=STAGE_B), 0:size] = part
+
+
+def lay_half(half, stage, mr_ref):
+    surface = mr_ref.shape[0]
     tiles = stage.shape[0]
     for j in range(4):
         for tile in range(tiles):
             rows = stage[tile, pl.ds(STAGE_B * (4 * half + j), surface, stride=STAGE_A), :]
             at = (j * tiles + tile) * LANES
-            for mr_ref in mr_refs:
-                mr_ref[:, at : at + LANES] = rows.astype(jnp.bfloat16)
+            mr_ref[:, at : at + LANES] = rows.astype(jnp.bfloat16)
 
 
 def gather_half(half, step, levels, idx_ref, tail_ref, table, g_ref):
@@ -343,7 +332,8 @@
             for q, value in gathered(tail_ref[at : at + CHUNK, :]):
                 put(target, q, body_lanes, jnp.where(lower, value, 0))
                 if target + upper < high:
-                    put(target + upper, q, body_lanes, jnp.where(lower, 0, value))
+                    moved = pltpu.roll(value, HALF, axis=1)
+                    put(target + upper, q, body_lanes, jnp.where(lower, moved, 0))
 
 
 def multiply(acc, g_ref, mr):
@@ -354,81 +344,6 @@
 
 def tail_rows(own):
     return ceil_to(own // CHUNK, 2) // 2 * CHUNK
-
-
-def local_kernel(
-    f_ref, idx_ref, tail_ref, m_ref, _, mr_ref, o_ref, table_f, table, unit, stage, acc, mr_b, g_a, g_b
-):
-    own = f_ref.shape[0]
-    half = mr_ref.shape[1] // 2
-    step = pl.program_id(0)
-
-    @pl.when(step == 0)
-    def _():
-        table_f[...] = f_ref[0:LOCAL, :].astype(jnp.float32).T
-        factor, unit[...] = scale_of(table_f[...])
-        table_f[...] = jnp.round(table_f[...] * factor)
-        pack_rows(table_f, table, 0)
-        acc[...] = jnp.zeros_like(acc)
-        mr_b[...] = jnp.zeros_like(mr_b)
-        g_b[...] = jnp.zeros_like(g_b)
-
-    levels = ((0, own, 0, 1, 0),)
-    stage_block(m_ref, stage)
-    lay_half(0, stage, mr_ref.at[:, 0:half])
-    multiply(acc, g_b, mr_b[...])
-    gather_half(0, step, levels, idx_ref, tail_ref, table, g_a)
-    lay_half(1, stage, mr_ref.at[:, half : 2 * half], mr_b)
-    multiply(acc, g_a, mr_ref[:, 0:half])
-    gather_half(1, step, levels, idx_ref, tail_ref, table, g_b)
-
-    @pl.when(step == pl.num_programs(0) - 1)
-    def _():
-        multiply(acc, g_b, mr_b[...])
-        o_ref[...] = acc[...] * unit[0:1, 0:1]
-
-
-def local_part(fine_rows, idx, tail, m2l_ops, after):
-    surface, _, offsets = m2l_ops.shape
-    width = ceil_to(offsets, LANES)
-    own = fine_rows.shape[0]
-    blocks = surface // 8
-    return pl.pallas_call(
-        local_kernel,
-        grid=(blocks,),
-        in_specs=[
-            whole(fine_rows),
-            whole(idx),
-            whole(tail),
-            pl.BlockSpec((surface, 8, offsets), lambda i: (0, i, 0)),
-            pl.BlockSpec(memory_space=pl.ANY),
-        ],
-        out_specs=[
-            pl.BlockSpec((None, surface, 8 * width), lambda i: (i, 0, 0)),
-            pl.BlockSpec((own, surface), lambda i: (0, 0)),
-        ],
-        out_shape=[
-            shape_of((blocks, surface, 8 * width), jnp.bfloat16),
-            shape_of((own, surface), jnp.float32),
-        ],
-        scratch_shapes=[
-            pltpu.VMEM((surface, LANES), jnp.float32),
-            pltpu.VMEM((blocks, 8, LANES), jnp.int32),
-            pltpu.VMEM((8, LANES), jnp.float32),
-            pltpu.VMEM((width // LANES, ceil_to(STAGE_A * surface, 8), LANES), jnp.float32),
-            pltpu.VMEM((own, surface), jnp.float32),
-            pltpu.VMEM((surface, 4 * width), jnp.bfloat16),
-            pltpu.VMEM((own, 4 * width), jnp.bfloat16),
-            pltpu.VMEM((own, 4 * width), jnp.bfloat16),
-        ],
-        compiler_params=pltpu.CompilerParams(vmem_limit_bytes=VMEM_BYTES),
-        cost_estimate=pl.CostEstimate(
-            flops=2 * surface * surface * own * width,
-            bytes_accessed=4 * surface * surface * width,
-            transcendentals=0,
-        ),
-        name="local_part",
-    )(fine_rows, idx, tail, m2l_ops, after)
 
 
 def translate_kernel(
@@ -441,9 +356,7 @@
     f_ref,
     c_ref,
     arrived_any,
-    part_ref,
-    ma_ref,
-    mb_ref,
+    m_ref,
     of_ref,
     oc_ref,
     rows_t,
@@ -451,21 +364,23 @@
     table,
     unit,
     arrived,
+    stage,
     acc,
+    mr_a,
+    mr_b,
     g_a,
     g_b,
     sem,
 ):
     fine_own, targets = of_ref.shape[0], idx_ref.shape[0]
     step = pl.program_id(0)
-    last = pl.num_programs(0) - 1
 
     @pl.when(step == 0)
     def _():
         fetch = pltpu.make_async_copy(arrived_any, arrived, sem)
         fetch.start()
-        acc[...] = jnp.zeros_like(acc)
-        g_b[...] = jnp.zeros_like(g_b)
+        for ref in (acc, stage, mr_b, g_b):
+            ref[...] = jnp.zeros_like(ref)
         fetch.wait()
         build_tables(
             ((0, coarse_tile), (coarse_tile, table_f.shape[0])),
@@ -484,30 +399,35 @@
             (0, fine_own, 0, fine_tiles, 0),
             (fine_own, targets, coarse_tile, coarse_tiles, tail_rows(fine_own)),
         )
-        multiply(acc, g_b, mb_ref[...])
+        stage_block(m_ref, stage)
+        lay_half(0, stage, mr_a)
+        multiply(acc, g_b, mr_b[...])
         gather_half(0, step, levels, idx_ref, tail_ref, table, g_a)
-        multiply(acc, g_a, ma_ref[...])
+        lay_half(1, stage, mr_b)
+        multiply(acc, g_a, mr_a[...])
         gather_half(1, step, levels, idx_ref, tail_ref, table, g_b)
 
     for at, tiles in enumerate(variants):
-        pl.when((pick_ref[0] == at) & (step < last))(functools.partial(work, *tiles))
-
-    @pl.when(step == last)
+        pl.when(pick_ref[0] == at)(functools.partial(work, *tiles))
+
+    @pl.when(step == pl.num_programs(0) - 1)
     def _():
-        multiply(acc, g_b, mb_ref[...])
-        of_ref[...] = acc[0:fine_own, :] * unit[0, 0:1, 0:1] + part_ref[...]
+        multiply(acc, g_b, mr_b[...])
+        of_ref[...] = acc[0:fine_own, :] * unit[0, 0:1, 0:1]
         oc_ref[...] = acc[fine_own:targets, :] * (0.5 * unit[1, 0:1, 0:1])
 
 
 def translate(
-    pick, idx, tail, to, fine_rows, coarse_rows, arrived, part, operators, variants, coarse_tile, tiles
+    pick, idx, tail, to, fine_rows, coarse_rows, arrived, m2l_ops, variants, coarse_tile, tiles
 ):
-    blocks, surface, depth = operators.shape
+    surface, _, offsets = m2l_ops.shape
+    width = ceil_to(offsets, LANES)
     targets = idx.shape[0]
     fine_own, coarse_own = fine_rows.shape[0], coarse_rows.shape[0]
+    blocks = surface // 8
     return pl.pallas_call(
         functools.partial(translate_kernel, variants, coarse_tile),
-        grid=(blocks + 1,),
+        grid=(blocks,),
         in_specs=[
             pl.BlockSpec(memory_space=pltpu.SMEM),
             whole(idx),
@@ -516,9 +436,7 @@
             whole(fine_rows),
             whole(coarse_rows),
             pl.BlockSpec(memory_space=pl.ANY),
-            whole(part),
-            pl.BlockSpec((None, surface, depth // 2), lambda i: (jnp.minimum(i, blocks - 1), 0, 0)),
-            pl.BlockSpec((None, surface, depth // 2), lambda i: (jnp.maximum(i - 1, 0), 0, 1)),
+            pl.BlockSpec((surface, 8, offsets), lambda i: (0, i, 0)),
         ],
         out_specs=[
             pl.BlockSpec((fine_own, surface), lambda i: (0, 0)),
@@ -534,19 +452,22 @@
             pltpu.VMEM((blocks, 8, tiles * LANES), jnp.int32),
             pltpu.VMEM((2, 8, LANES), jnp.float32),
             pltpu.VMEM(arrived.shape, jnp.bfloat16),
+            pltpu.VMEM((width // LANES, ceil_to(STAGE_A * surface, 8), LANES), jnp.float32),
             pltpu.VMEM((targets, surface), jnp.float32),
-            pltpu.VMEM((targets, depth // 2), jnp.bfloat16),
-            pltpu.VMEM((targets, depth // 2), jnp.bfloat16),
+            pltpu.VMEM((surface, 4 * width), jnp.bfloat16),
+            pltpu.VMEM((surface, 4 * width), jnp.bfloat16),
+            pltpu.VMEM((targets, 4 * width), jnp.bfloat16),
+            pltpu.VMEM((targets, 4 * width), jnp.bfloat16),
             pltpu.SemaphoreType.DMA,
         ],
         compiler_params=pltpu.CompilerParams(vmem_limit_bytes=VMEM_BYTES),
         cost_estimate=pl.CostEstimate(
-            flops=blocks * surface * targets * depth * 2,
-            bytes_accessed=2 * blocks * surface * depth,
+            flops=2 * surface * surface * targets * width,
+            bytes_accessed=2 * surface * surface * width,
             transcendentals=0,
         ),
         name="translate",
-    )(pick, idx, tail, to, fine_rows, coarse_rows, arrived, part, operators, operators)
+    )(pick, idx, tail, to, fine_rows, coarse_rows, arrived, m2l_ops)
 
 
 def exchange(x):
@@ -565,9 +486,9 @@
 
     fine_tiles = ceil_to(fine_own - LOCAL + (peers - 1) * fine_cap, LANES) // LANES
     coarse_tiles = ceil_to(coarse_own + (peers - 1) * coarse_cap, LANES) // LANES
-    variants = [(min(n, fine_tiles), min(2, coarse_tiles)) for n in (2, 3)]
+    variants = [(min(n, fine_tiles), min(2, coarse_tiles)) for n in (3, 4)]
     variants = variants + [(fine_tiles, coarse_tiles)]
-    idx, tail, to, pick, own_idx, own_tail = plan(
+    idx, tail, to, pick = plan(
         asks_fine, asks_coarse, list_fine, list_coarse, variants, fine_tiles * LANES
     )
 
@@ -593,7 +514,6 @@
     )
 
     arrived = exchange(answer(wanted, fine_rows, coarse_rows))
-    operators, part = local_part(fine_rows, own_idx, own_tail, m2l_ops, wanted)
     pot_fine, pot_coarse = translate(
         pick,
         idx,
@@ -602,8 +522,7 @@
         fine_rows,
         coarse_rows,
         arrived,
-        part,
-        operators,
+        m2l_ops,
         variants,
         fine_tiles,
         fine_tiles + coarse_tiles,

time: 86.9 us -> 98.7 us (1.14)
  the two profiles are of different devices: /device:TPU:13 before, /device:TPU:8 now
where the time goes in v1:
time: 98.7 us; the launch traced here: 97.1 us
  Pallas kernels  72 us (73%)
  starting transfers between devices  9.88 us (10%)
  waiting for transfers between devices  9.47 us (10%)
  other arithmetic  2.55 us (3%)
  local copies, waits for them, and re-layouts  1.32 us (1%)
  matrix products  1.2 us (1%)
    pallas_call x1, Pallas kernels, translate(): pl.pallas_call(functools.partial(translate_kernel, variants, coarse_tile)...  65.5 us
    all_to_all x2, starting transfers between devices, exchange(): return lax.all_to_all(x, AXES, split_axis=0, concat_axis=0, tiled=True)  9.88 us
    all_to_all x2, waiting for transfers between devices, exchange(): return lax.all_to_all(x, AXES, split_axis=0, concat_axis=0, tiled=True)  9.47 us
    pallas_call x1, Pallas kernels, answer(): pl.pallas_call(answer_kernel, in_specs=[whole(wanted), whole(fine_rows),...  2.65 us
    pallas_call x1, Pallas kernels, plan(): pl.pallas_call(functools.partial(plan_kernel, variants, coarse_at), out_s...  2.38 us
  transfers between devices with their start and end apart: 2, of which 2 were waited for; matrix products, arithmetic and copies ran while one was open for 4% of the time, Pallas kernels for 2%

profile of v1, /device:TPU:8, one launch (start us, length us, event | category | flops | bytes accessed | tf_op | source)
XLA Modules:
  0.0 97.1 jit_solution(16874368500082957453)
XLA Ops:
  0.6 0.0 copy-start
  0.6 1.5 %join_asks.1 = s32[32,24]{1,0:T(8,128)} custom-call(s32[16,32]{1,0:T(8,128)} %bitcast.21, s32[8,32]{1,0:T(8,128)} %bitcast.23), custom_call_target="tpu_custom_call" | custom-call | tf_op jit(solution)/shard_map/join_asks/pallas_call | solution.py:49
  2.1 6.0 %all-to-all-start = ((s32[32,1,24]{2,1,0:T(1,128)}), s32[32,1,24]{2,1,0:T(1,128)S(1)}, u32[]{:S(2)}, u32[]{:S(2)}) async-start(s32[32,1,24]{2,1,0:T(1,128)} %bitcast.20), calls=%async_computation | async-start | bytes 32768 | tf_op jit(solution)/shard_map/all_to_all | solution.py:474
  8.2 0.8 iota_compare_fusion
  8.9 0.7 broadcast_subtract_fusion
  9.6 1.1 %broadcast_select_fusion = bf16[144,8,152]{2,1,0:T(8,128)(2,1)S(1)} fusion(pred[144,8]{1,0:T(8,128)(4,1)S(1)} %iota_compare_fusion, bf16[144,152]{1,0:T(8,128)(2,1)} %bitcast.16), kind=kLoop, calls=%fused_computation.4 | loop fusion | flops 175104 | bytes 395136 | tf_op jit(solution)/shard_map/jit(_where)/select_n | solution.py:497
  10.7 0.0 copy-done
  10.7 0.4 convolution_bitcast_fusion
  11.2 0.8 convolution_convert_fusion.c_any.c_ref
  11.9 2.0 %all-to-all-done = s32[32,1,24]{2,1,0:T(1,128)S(1)} async-done(((s32[32,1,24]{2,1,0:T(1,128)}), s32[32,1,24]{2,1,0:T(1,128)S(1)}, u32[]{:S(2)}, u32[]{:S(2)}) %all-to-all-start) | async-done | bytes 3104 | tf_op jit(solution)/shard_map/all_to_all | solution.py:474
  14.0 0.0 copy-start.2
  14.0 0.6 copy-done.2
  14.6 2.7 %answer.1 = bf16[32,32,128]{2,1,0:T(8,128)(2,1)} custom-call(s32[32,24]{1,0:T(8,128)} %bitcast.19, bf16[144,152]{1,0:T(8,128)(2,1)} %bitcast.17, bf16[32,152]{1,0:T(8,128)(2,1)} %convolution_convert_fusion.c_any.c_ref), custom_call_target="tpu_custom_call" | custom-call | tf_op jit(solution)/shard_map/answer/pallas_call | solution.py:90
  17.2 3.8 %all-to-all-start.1 = ((bf16[32,32,128]{2,1,0:T(8,128)(2,1)}), bf16[32,32,128]{2,1,0:T(8,128)(2,1)S(1)}, u32[]{:S(2)}, u32[]{:S(2)}) async-start(bf16[32,32,128]{2,1,0:T(8,128)(2,1)} %answer.1), calls=%async_computation.1 | async-start | bytes 524288 | tf_op jit(solution)/shard_map/all_to_all | solution.py:474
  21.1 2.4 %plan.1 = (s32[176,256]{1,0:T(8,128)}, s32[96,128]{1,0:T(8,128)}, s32[944,128]{1,0:T(8,128)}, s32[1]{0:T(128)}) custom-call(s32[16,32]{1,0:T(8,128)} %bitcast.22, s32[8,32]{1,0:T(8,128)} %bitcast.24, s32[144,316]{1,0:T(8,128)} %lf_ref.1, s32[32,316]{1,0:T(8,128)} %lc_ref.1), custom_call_target="tpu_custom_call" | custom-call | tf_op jit(solution)/shard_map/plan/pallas_call | solution.py:209
  23.4 7.5 %all-to-all-done.1.arrived_any = bf16[32,32,128]{2,1,0:T(8,128)(2,1)S(1)} async-done(((bf16[32,32,128]{2,1,0:T(8,128)(2,1)}), bf16[32,32,128]{2,1,0:T(8,128)(2,1)S(1)}, u32[]{:S(2)}, u32[]{:S(2)}) %all-to-all-start.1) | async-done | bytes 262176 | tf_op jit(solution)/shard_map/all_to_all | solution.py:474
  30.9 0.0 copy-start.1
  30.9 0.7 copy-done.1
  31.6 65.5 %translate.1 = (f32[144,152]{1,0:T(8,128)}, f32[32,152]{1,0:T(8,128)}) custom-call(s32[1]{0:T(128)} %get-tuple-element.8.pick_ref, s32[176,256]{1,0:T(8,128)} %get-tuple-element.9.idx_ref, s32[96,128]{1,0:T(8,128)} %get-tuple-element.10.tail_ref, s32[944,128]{1,0:T(8,128)} %get-tuple-element.11.to_ref, bf16[144,152]{1,0:T(8,128)(2,1)} %bitcast.18, ...), custom_call_target="tpu_custom_call" | custom-call | flops 3122921472 | bytes 17743872 | tf_op jit(solution)/shard_map/translate/pallas_call | solution.py:428
Async XLA Ops:
  0.6 10.1 %copy-start = (bf16[152,8,152]{2,1,0:T(8,128)(2,1)S(1)}, bf16[152,8,152]{2,1,0:T(8,128)(2,1)}, u32[]{:S(2)}) copy-start(bf16[152,8,152]{2,1,0:T(8,128)(2,1)} %param.12) | copy-start | bytes 1108996
  2.1 11.9 %all-to-all-start = ((s32[32,1,24]{2,1,0:T(1,128)}), s32[32,1,24]{2,1,0:T(1,128)S(1)}, u32[]{:S(2)}, u32[]{:S(2)}) async-start(s32[32,1,24]{2,1,0:T(1,128)} %bitcast.20), calls=%async_computation | async-start | bytes 32768 | tf_op jit(solution)/shard_map/all_to_all | solution.py:474
  14.0 0.6 copy-start.2
  17.2 13.7 %all-to-all-start.1 = ((bf16[32,32,128]{2,1,0:T(8,128)(2,1)}), bf16[32,32,128]{2,1,0:T(8,128)(2,1)S(1)}, u32[]{:S(2)}, u32[]{:S(2)}) async-start(bf16[32,32,128]{2,1,0:T(8,128)(2,1)} %answer.1), calls=%async_computation.1 | async-start | bytes 524288 | tf_op jit(solution)/shard_map/all_to_all | solution.py:474
  30.9 0.7 copy-start.1

commit v2 on v1

--- a/solution.py
+++ b/solution.py
@@ -9,8 +9,7 @@
 
 LANES = 128
 CHUNK = 16
-HALF = LANES // 2
-BLANK = 1 << 20
+BLANK = -1
 LOCAL = 0
 AXES = ("leaf", "oct")
 STAGE_A, STAGE_B = 23, 3
@@ -97,6 +96,7 @@
             pltpu.VMEM(coarse_rows.shape, jnp.bfloat16),
             pltpu.SemaphoreType.DMA,
         ],
+        compiler_params=pltpu.CompilerParams(vmem_limit_bytes=16 << 20),
         name="answer",
     )(wanted, fine_rows, coarse_rows)
 
@@ -119,19 +119,18 @@
     lf_ref,
     lc_ref,
     idx_ref,
-    tail_ref,
     to_ref,
     pick_ref,
     cnt,
 ):
     offsets = lf_ref.shape[1]
-    body_lanes = idx_ref.shape[1]
+    body_lanes = offsets // LANES * LANES
     peers = af_ref.shape[1]
     lanes = lane_iota((LANES, LANES))
     earlier = lax.broadcasted_iota(jnp.int32, (LANES, LANES), 0) < lanes
     earlier = earlier.astype(jnp.float32).astype(jnp.bfloat16)
     levels = []
-    row = tail_row = 0
+    row = 0
     cnt[...] = jnp.zeros_like(cnt)
     for level, (ask_ref, list_ref) in enumerate(((af_ref, lf_ref), (ac_ref, lc_ref))):
         own, cap = list_ref.shape[0], ask_ref.shape[0]
@@ -156,23 +155,11 @@
                 axis=1,
             )
         )
-        upper = tail_rows(own)
-
-        def keep(columns, to_body, to_tail, at, tail_at):
-            for k, x in enumerate(columns[:-1]):
-                to_body[at : at + own, k * LANES : (k + 1) * LANES] = x
-            rest = columns[-1]
-            moved = pltpu.roll(rest[upper:], HALF, axis=1)
-            if own - upper < upper:
-                missing = jnp.full((2 * upper - own, LANES), BLANK, jnp.int32)
-                moved = jnp.concatenate([moved, missing], axis=0)
-            to_tail[tail_at : tail_at + upper, :] = jnp.where(
-                lane_iota((upper, LANES)) < HALF, rest[0:upper], moved
+        for k, x in enumerate(lists):
+            idx_ref[row : row + own, k * LANES : (k + 1) * LANES] = remap(
+                x, own, done, cap, shift
             )
-
-        keep([remap(x, own, done, cap, shift) for x in lists], idx_ref, tail_ref, row, tail_row)
         row += own
-        tail_row += upper
 
     (fine_own, fine_cap, *fine), (coarse_own, coarse_cap, *coarse) = levels
     place = lax.broadcasted_iota(jnp.int32, (8, LANES), 0)
@@ -202,16 +189,14 @@
 
 def plan(asks_fine, asks_coarse, list_fine, list_coarse, variants, coarse_at):
     own = list_fine.shape[0] + list_coarse.shape[0]
-    tails = sum(tail_rows(x.shape[0]) for x in (list_fine, list_coarse))
-    body_lanes = list_fine.shape[1] // LANES * LANES
+    width = ceil_to(list_fine.shape[1], LANES)
     slots, peers = asks_fine.shape[0] + asks_coarse.shape[0], asks_fine.shape[1]
     vmem = pl.BlockSpec(memory_space=pltpu.VMEM)
     return pl.pallas_call(
         functools.partial(plan_kernel, variants, coarse_at),
-        out_specs=[vmem, vmem, vmem, pl.BlockSpec(memory_space=pltpu.SMEM)],
+        out_specs=[vmem, vmem, pl.BlockSpec(memory_space=pltpu.SMEM)],
         out_shape=[
-            shape_of((own, body_lanes), jnp.int32),
-            shape_of((tails, LANES), jnp.int32),
+            shape_of((own, width), jnp.int32),
             shape_of((own + peers * slots, LANES), jnp.int32),
             shape_of((1,), jnp.int32),
         ],
@@ -267,13 +252,15 @@
             pack_rows(table_f.at[k], table, k)
 
 
-def stage_block(m_ref, stage):
-    surface, _, offsets = m_ref.shape
-    for tile, first in enumerate(range(0, offsets, LANES)):
-        size = min(LANES, offsets - first)
+def stage_block(offsets, m_ref, stage):
+    surface, _, width = m_ref.shape
+    for tile, first in enumerate(range(0, width, LANES)):
+        inside = lane_iota((8, LANES)) < offsets - first
         for a in range(surface):
-            part = m_ref[a, :, first : first + size].astype(jnp.float32)
-            stage[tile, pl.ds(STAGE_A * a, 8, stride=STAGE_B), 0:size] = part
+            part = m_ref[a, :, first : first + LANES].astype(jnp.float32)
+            if first + LANES > offsets:
+                part = jnp.where(inside, part, 0.0)
+            stage[tile, pl.ds(STAGE_A * a, 8, stride=STAGE_B), :] = part
 
 
 def lay_half(half, stage, mr_ref):
@@ -286,19 +273,9 @@
             mr_ref[:, at : at + LANES] = rows.astype(jnp.bfloat16)
 
 
-def gather_half(half, step, levels, idx_ref, tail_ref, table, g_ref):
-    body_lanes = idx_ref.shape[1]
-    width = body_lanes + LANES
-    lower = lane_iota((CHUNK, LANES)) < HALF
-
-    def put(rows, q, at, value):
-        to = 2 * q * width + at
-        low = (value << 16).astype(jnp.float32).astype(jnp.bfloat16)
-        high = value.astype(jnp.float32).astype(jnp.bfloat16)
-        g_ref[rows : rows + CHUNK, to : to + LANES] = low
-        g_ref[rows : rows + CHUNK, to + width : to + width + LANES] = high
-
-    for low, high, base, tiles, tail_row in levels:
+def gather_half(half, step, levels, idx_ref, table, g_ref):
+    width = idx_ref.shape[1]
+    for low, high, base, tiles in levels:
         rows = [
             [
                 jnp.broadcast_to(
@@ -309,31 +286,21 @@
             ]
             for pair in (2 * half, 2 * half + 1)
         ]
-
-        def gathered(idx):
-            at = idx & (LANES - 1)
-            later = [idx >= k * LANES for k in range(1, tiles)]
-            blank = idx >= BLANK
-            for q in range(2):
-                value = None
-                for k in range(tiles):
-                    got = jnp.take_along_axis(rows[q][k], at, axis=1, mode="promise_in_bounds")
-                    value = got if k == 0 else jnp.where(later[k - 1], got, value)
-                yield q, jnp.where(blank, 0, value)
-
-        for first in range(0, body_lanes, LANES):
+        for first in range(0, width, LANES):
             for target in range(low, high, CHUNK):
                 idx = idx_ref[target : target + CHUNK, first : first + LANES]
-                for q, value in gathered(idx):
-                    put(target, q, first, value)
-        upper = tail_rows(high - low)
-        for target in range(low, low + upper, CHUNK):
-            at = tail_row + target - low
-            for q, value in gathered(tail_ref[at : at + CHUNK, :]):
-                put(target, q, body_lanes, jnp.where(lower, value, 0))
-                if target + upper < high:
-                    moved = pltpu.roll(value, HALF, axis=1)
-                    put(target + upper, q, body_lanes, jnp.where(lower, moved, 0))
+                at = idx & (LANES - 1)
+                inside = [idx >= k * LANES for k in range(tiles)]
+                for q in range(2):
+                    value = jnp.zeros((CHUNK, LANES), jnp.int32)
+                    for k in range(tiles):
+                        got = jnp.take_along_axis(rows[q][k], at, axis=1, mode="promise_in_bounds")
+                        value = jnp.where(inside[k], got, value)
+                    low_half = (value << 16).astype(jnp.float32).astype(jnp.bfloat16)
+                    high_half = value.astype(jnp.float32).astype(jnp.bfloat16)
+                    to = 2 * q * width + first
+                    g_ref[target : target + CHUNK, to : to + LANES] = low_half
+                    g_ref[target : target + CHUNK, to + width : to + width + LANES] = high_half
 
 
 def multiply(acc, g_ref, mr):
@@ -342,16 +309,12 @@
     )
 
 
-def tail_rows(own):
-    return ceil_to(own // CHUNK, 2) // 2 * CHUNK
-
-
 def translate_kernel(
     variants,
     coarse_tile,
+    offsets,
     pick_ref,
     idx_ref,
-    tail_ref,
     to_ref,
     f_ref,
     c_ref,
@@ -379,7 +342,7 @@
     def _():
         fetch = pltpu.make_async_copy(arrived_any, arrived, sem)
         fetch.start()
-        for ref in (acc, stage, mr_b, g_b):
+        for ref in (acc, mr_b, g_b):
             ref[...] = jnp.zeros_like(ref)
         fetch.wait()
         build_tables(
@@ -396,16 +359,16 @@
 
     def work(fine_tiles, coarse_tiles):
         levels = (
-            (0, fine_own, 0, fine_tiles, 0),
-            (fine_own, targets, coarse_tile, coarse_tiles, tail_rows(fine_own)),
+            (0, fine_own, 0, fine_tiles),
+            (fine_own, targets, coarse_tile, coarse_tiles),
         )
-        stage_block(m_ref, stage)
+        stage_block(offsets, m_ref, stage)
         lay_half(0, stage, mr_a)
         multiply(acc, g_b, mr_b[...])
-        gather_half(0, step, levels, idx_ref, tail_ref, table, g_a)
+        gather_half(0, step, levels, idx_ref, table, g_a)
         lay_half(1, stage, mr_b)
         multiply(acc, g_a, mr_a[...])
-        gather_half(1, step, levels, idx_ref, tail_ref, table, g_b)
+        gather_half(1, step, levels, idx_ref, table, g_b)
 
     for at, tiles in enumerate(variants):
         pl.when(pick_ref[0] == at)(functools.partial(work, *tiles))
@@ -418,7 +381,7 @@
 
 
 def translate(
-    pick, idx, tail, to, fine_rows, coarse_rows, arrived, m2l_ops, variants, coarse_tile, tiles
+    pick, idx, to, fine_rows, coarse_rows, arrived, m2l_ops, variants, coarse_tile, tiles
 ):
     surface, _, offsets = m2l_ops.shape
     width = ceil_to(offsets, LANES)
@@ -426,17 +389,16 @@
     fine_own, coarse_own = fine_rows.shape[0], coarse_rows.shape[0]
     blocks = surface // 8
     return pl.pallas_call(
-        functools.partial(translate_kernel, variants, coarse_tile),
+        functools.partial(translate_kernel, variants, coarse_tile, offsets),
         grid=(blocks,),
         in_specs=[
             pl.BlockSpec(memory_space=pltpu.SMEM),
             whole(idx),
-            whole(tail),
             whole(to),
             whole(fine_rows),
             whole(coarse_rows),
             pl.BlockSpec(memory_space=pl.ANY),
-            pl.BlockSpec((surface, 8, offsets), lambda i: (0, i, 0)),
+            pl.BlockSpec((surface, 8, width), lambda i: (0, i, 0)),
         ],
         out_specs=[
             pl.BlockSpec((fine_own, surface), lambda i: (0, 0)),
@@ -467,7 +429,7 @@
             transcendentals=0,
         ),
         name="translate",
-    )(pick, idx, tail, to, fine_rows, coarse_rows, arrived, m2l_ops)
+    )(pick, idx, to, fine_rows, coarse_rows, arrived, m2l_ops)
 
 
 def exchange(x):
@@ -488,7 +450,7 @@
     coarse_tiles = ceil_to(coarse_own + (peers - 1) * coarse_cap, LANES) // LANES
     variants = [(min(n, fine_tiles), min(2, coarse_tiles)) for n in (3, 4)]
     variants = variants + [(fine_tiles, coarse_tiles)]
-    idx, tail, to, pick = plan(
+    idx, to, pick = plan(
         asks_fine, asks_coarse, list_fine, list_coarse, variants, fine_tiles * LANES
     )
 
@@ -517,7 +479,6 @@
     pot_fine, pot_coarse = translate(
         pick,
         idx,
-        tail,
         to,
         fine_rows,
         coarse_rows,

time: 98.7 us -> 81 us (0.82)
  the two profiles are of different devices: /device:TPU:8 before, /device:TPU:5 now
where the time goes in v2:
time: 81 us; the launch traced here: 80.6 us
  Pallas kernels  54.8 us (68%)
  starting transfers between devices  10.4 us (13%)
  waiting for transfers between devices  9.96 us (12%)
  other arithmetic  2.55 us (3%)
  local copies, waits for them, and re-layouts  1.6 us (2%)
    pallas_call x1, Pallas kernels, translate(): pl.pallas_call(functools.partial(translate_kernel, variants, coarse_tile,...  49.6 us
    all_to_all x2, starting transfers between devices, exchange(): return lax.all_to_all(x, AXES, split_axis=0, concat_axis=0, tiled=True)  10.4 us
    all_to_all x2, waiting for transfers between devices, exchange(): return lax.all_to_all(x, AXES, split_axis=0, concat_axis=0, tiled=True)  9.96 us
    pallas_call x1, Pallas kernels, plan(): pl.pallas_call(functools.partial(plan_kernel, variants, coarse_at), out_s...  2.37 us
  transfers between devices with their start and end apart: 2, of which 2 were waited for; matrix products, arithmetic and copies ran while one was open for 4% of the time, Pallas kernels for 3%

profile of v2, /device:TPU:5, one launch (start us, length us, event | category | flops | bytes accessed | tf_op | source)
XLA Modules:
  0.0 80.6 jit_solution(18270399922783480459)
XLA Ops:
  0.6 0.0 copy-start
  0.6 1.5 %join_asks.1 = s32[32,24]{1,0:T(8,128)} custom-call(s32[16,32]{1,0:T(8,128)} %bitcast.21, s32[8,32]{1,0:T(8,128)} %bitcast.23), custom_call_target="tpu_custom_call" | custom-call | tf_op jit(solution)/shard_map/join_asks/pallas_call | solution.py:48
  2.1 6.4 %all-to-all-start = ((s32[32,1,24]{2,1,0:T(1,128)}), s32[32,1,24]{2,1,0:T(1,128)S(1)}, u32[]{:S(2)}, u32[]{:S(2)}) async-start(s32[32,1,24]{2,1,0:T(1,128)} %bitcast.20), calls=%async_computation | async-start | bytes 32768 | tf_op jit(solution)/shard_map/all_to_all | solution.py:436
  8.5 0.8 iota_compare_fusion
  9.3 0.7 broadcast_subtract_fusion
  10.0 1.1 %broadcast_select_fusion = bf16[144,8,152]{2,1,0:T(8,128)(2,1)S(1)} fusion(pred[144,8]{1,0:T(8,128)(4,1)S(1)} %iota_compare_fusion, bf16[144,152]{1,0:T(8,128)(2,1)} %bitcast.16), kind=kLoop, calls=%fused_computation.4 | loop fusion | flops 175104 | bytes 395136 | tf_op jit(solution)/shard_map/jit(_where)/select_n | solution.py:459
  11.1 0.0 copy-done
  11.1 0.4 convolution_bitcast_fusion
  11.5 0.2 convolution_convert_fusion.c_any.c_ref
  11.7 0.0 copy-start.2
  11.7 2.4 %all-to-all-done = s32[32,1,24]{2,1,0:T(1,128)S(1)} async-done(((s32[32,1,24]{2,1,0:T(1,128)}), s32[32,1,24]{2,1,0:T(1,128)S(1)}, u32[]{:S(2)}, u32[]{:S(2)}) %all-to-all-start) | async-done | bytes 3104 | tf_op jit(solution)/shard_map/all_to_all | solution.py:436
  14.1 0.0 copy-start.1
  14.1 0.9 %copy-done.1 = bf16[152,144]{0,1:T(8,128)(2,1)S(1)} copy-done((bf16[152,144]{0,1:T(8,128)(2,1)S(1)}, bf16[152,144]{0,1:T(8,128)(2,1)}, u32[]{:S(2)}) %copy-start.1) | copy-done | bytes 43800
  15.0 1.4 %answer.1 = bf16[32,32,128]{2,1,0:T(8,128)(2,1)} custom-call(s32[32,24]{1,0:T(8,128)S(1)} %bitcast.19, bf16[144,152]{1,0:T(8,128)(2,1)S(1)} %bitcast.18, bf16[32,152]{1,0:T(8,128)(2,1)S(1)} %convolution_convert_fusion.c_any.c_ref), custom_call_target="tpu_custom_call" | custom-call | tf_op jit(solution)/shard_map/answer/pallas_call | solution.py:89
  16.3 4.0 %all-to-all-start.1 = ((bf16[32,32,128]{2,1,0:T(8,128)(2,1)}), bf16[32,32,128]{2,1,0:T(8,128)(2,1)S(1)}, u32[]{:S(2)}, u32[]{:S(2)}) async-start(bf16[32,32,128]{2,1,0:T(8,128)(2,1)} %answer.1), calls=%async_computation.1 | async-start | bytes 524288 | tf_op jit(solution)/shard_map/all_to_all | solution.py:436
  20.3 2.4 %plan.1 = (s32[176,384]{1,0:T(8,128)}, s32[944,128]{1,0:T(8,128)}, s32[1]{0:T(128)}) custom-call(s32[16,32]{1,0:T(8,128)} %bitcast.22, s32[8,32]{1,0:T(8,128)} %bitcast.24, s32[144,316]{1,0:T(8,128)} %lf_ref.1, s32[32,316]{1,0:T(8,128)} %lc_ref.1), custom_call_target="tpu_custom_call" | custom-call | tf_op jit(solution)/shard_map/plan/pallas_call | solution.py:195
  22.7 7.6 %all-to-all-done.1.arrived_any = bf16[32,32,128]{2,1,0:T(8,128)(2,1)S(1)} async-done(((bf16[32,32,128]{2,1,0:T(8,128)(2,1)}), bf16[32,32,128]{2,1,0:T(8,128)(2,1)S(1)}, u32[]{:S(2)}, u32[]{:S(2)}) %all-to-all-start.1) | async-done | bytes 262176 | tf_op jit(solution)/shard_map/all_to_all | solution.py:436
  30.3 0.0 copy-start.3
  30.3 0.0 copy-done.2
  30.3 0.7 copy-done.3
  31.0 49.6 %translate.1 = (f32[144,152]{1,0:T(8,128)}, f32[32,152]{1,0:T(8,128)}) custom-call(s32[1]{0:T(128)} %get-tuple-element.7.pick_ref, s32[176,384]{1,0:T(8,128)} %get-tuple-element.8.idx_ref, s32[944,128]{1,0:T(8,128)} %get-tuple-element.9.to_ref, bf16[144,152]{1,0:T(8,128)(2,1)} %bitcast.17, bf16[32,152]{1,0:T(8,128)(2,1)} %copy-done.2, ...), custom_call_target="tpu_custom_call" | custom-call | flops 3122921472 | bytes 17743872 | tf_op jit(solution)/shard_map/translate/pallas_call | solution.py:391
Async XLA Ops:
  0.6 10.5 %copy-start = (bf16[152,8,152]{2,1,0:T(8,128)(2,1)S(1)}, bf16[152,8,152]{2,1,0:T(8,128)(2,1)}, u32[]{:S(2)}) copy-start(bf16[152,8,152]{2,1,0:T(8,128)(2,1)} %param.12) | copy-start | bytes 1108996
  2.1 12.0 %all-to-all-start = ((s32[32,1,24]{2,1,0:T(1,128)}), s32[32,1,24]{2,1,0:T(1,128)S(1)}, u32[]{:S(2)}, u32[]{:S(2)}) async-start(s32[32,1,24]{2,1,0:T(1,128)} %bitcast.20), calls=%async_computation | async-start | bytes 32768 | tf_op jit(solution)/shard_map/all_to_all | solution.py:436
  11.7 18.6 %copy-start.2 = (bf16[32,152]{1,0:T(8,128)(2,1)}, bf16[32,152]{1,0:T(8,128)(2,1)S(1)}, u32[]{:S(2)}) copy-start(bf16[32,152]{1,0:T(8,128)(2,1)S(1)} %convolution_convert_fusion.c_any.c_ref) | copy-start | bytes 29188
  14.1 0.9 %copy-start.1 = (bf16[152,144]{0,1:T(8,128)(2,1)S(1)}, bf16[152,144]{0,1:T(8,128)(2,1)}, u32[]{:S(2)}) copy-start(bf16[152,144]{0,1:T(8,128)(2,1)} %param.9) | copy-start | bytes 131332
  16.3 13.9 %all-to-all-start.1 = ((bf16[32,32,128]{2,1,0:T(8,128)(2,1)}), bf16[32,32,128]{2,1,0:T(8,128)(2,1)S(1)}, u32[]{:S(2)}, u32[]{:S(2)}) async-start(bf16[32,32,128]{2,1,0:T(8,128)(2,1)} %answer.1), calls=%async_computation.1 | async-start | bytes 524288 | tf_op jit(solution)/shard_map/all_to_all | solution.py:436
  30.3 0.7 copy-start.3

commit v3 on v2

--- a/solution.py
+++ b/solution.py
@@ -263,39 +263,49 @@
             stage[tile, pl.ds(STAGE_A * a, 8, stride=STAGE_B), :] = part
 
 
-def lay_half(half, stage, mr_ref):
+def lay_block(stage, mr_ref):
     surface = mr_ref.shape[0]
     tiles = stage.shape[0]
-    for j in range(4):
+    for j in range(8):
         for tile in range(tiles):
-            rows = stage[tile, pl.ds(STAGE_B * (4 * half + j), surface, stride=STAGE_A), :]
+            rows = stage[tile, pl.ds(STAGE_B * j, surface, stride=STAGE_A), :]
             at = (j * tiles + tile) * LANES
             mr_ref[:, at : at + LANES] = rows.astype(jnp.bfloat16)
 
 
-def gather_half(half, step, levels, idx_ref, table, g_ref):
+def gather_block(step, levels, idx_ref, table, g_ref):
     width = idx_ref.shape[1]
     for low, high, base, tiles in levels:
         rows = [
             [
                 jnp.broadcast_to(
-                    table[step, pair : pair + 1, (base + k) * LANES : (base + k + 1) * LANES],
-                    (CHUNK, LANES),
+                    table[step, q : q + 1, (base + k) * LANES : (base + k + 1) * LANES],
+                    (8, LANES),
                 )
                 for k in range(tiles)
             ]
-            for pair in (2 * half, 2 * half + 1)
+            for q in range(4)
         ]
+
+        def words(target, first):
+            idx = idx_ref[target : target + 8, first : first + LANES]
+            at = idx & (LANES - 1)
+            later = [idx >= k * LANES for k in range(1, tiles)]
+            blank = idx < 0
+            values = []
+            for q in range(4):
+                value = None
+                for k in range(tiles):
+                    got = jnp.take_along_axis(rows[q][k], at, axis=1, mode="promise_in_bounds")
+                    value = got if k == 0 else jnp.where(later[k - 1], got, value)
+                values.append(jnp.where(blank, 0, value))
+            return values
+
         for first in range(0, width, LANES):
             for target in range(low, high, CHUNK):
-                idx = idx_ref[target : target + CHUNK, first : first + LANES]
-                at = idx & (LANES - 1)
-                inside = [idx >= k * LANES for k in range(tiles)]
-                for q in range(2):
-                    value = jnp.zeros((CHUNK, LANES), jnp.int32)
-                    for k in range(tiles):
-                        got = jnp.take_along_axis(rows[q][k], at, axis=1, mode="promise_in_bounds")
-                        value = jnp.where(inside[k], got, value)
+                upper, lower = words(target, first), words(target + 8, first)
+                for q in range(4):
+                    value = jnp.concatenate([upper[q], lower[q]], axis=0)
                     low_half = (value << 16).astype(jnp.float32).astype(jnp.bfloat16)
                     high_half = value.astype(jnp.float32).astype(jnp.bfloat16)
                     to = 2 * q * width + first
@@ -329,10 +339,8 @@
     arrived,
     stage,
     acc,
-    mr_a,
-    mr_b,
-    g_a,
-    g_b,
+    mr,
+    g,
     sem,
 ):
     fine_own, targets = of_ref.shape[0], idx_ref.shape[0]
@@ -342,7 +350,7 @@
     def _():
         fetch = pltpu.make_async_copy(arrived_any, arrived, sem)
         fetch.start()
-        for ref in (acc, mr_b, g_b):
+        for ref in (acc, mr, g):
             ref[...] = jnp.zeros_like(ref)
         fetch.wait()
         build_tables(
@@ -362,20 +370,17 @@
             (0, fine_own, 0, fine_tiles),
             (fine_own, targets, coarse_tile, coarse_tiles),
         )
+        multiply(acc, g, mr[...])
         stage_block(offsets, m_ref, stage)
-        lay_half(0, stage, mr_a)
-        multiply(acc, g_b, mr_b[...])
-        gather_half(0, step, levels, idx_ref, table, g_a)
-        lay_half(1, stage, mr_b)
-        multiply(acc, g_a, mr_a[...])
-        gather_half(1, step, levels, idx_ref, table, g_b)
+        lay_block(stage, mr)
+        gather_block(step, levels, idx_ref, table, g)
 
     for at, tiles in enumerate(variants):
         pl.when(pick_ref[0] == at)(functools.partial(work, *tiles))
 
     @pl.when(step == pl.num_programs(0) - 1)
     def _():
-        multiply(acc, g_b, mr_b[...])
+        multiply(acc, g, mr[...])
         of_ref[...] = acc[0:fine_own, :] * unit[0, 0:1, 0:1]
         oc_ref[...] = acc[fine_own:targets, :] * (0.5 * unit[1, 0:1, 0:1])
 
@@ -416,10 +421,8 @@
             pltpu.VMEM(arrived.shape, jnp.bfloat16),
             pltpu.VMEM((width // LANES, ceil_to(STAGE_A * surface, 8), LANES), jnp.float32),
             pltpu.VMEM((targets, surface), jnp.float32),
-            pltpu.VMEM((surface, 4 * width), jnp.bfloat16),
-            pltpu.VMEM((surface, 4 * width), jnp.bfloat16),
-            pltpu.VMEM((targets, 4 * width), jnp.bfloat16),
-            pltpu.VMEM((targets, 4 * width), jnp.bfloat16),
+            pltpu.VMEM((surface, 8 * width), jnp.bfloat16),
+            pltpu.VMEM((targets, 8 * width), jnp.bfloat16),
             pltpu.SemaphoreType.DMA,
         ],
         compiler_params=pltpu.CompilerParams(vmem_limit_bytes=VMEM_BYTES),

time: 81 us -> 64.8 us (0.80)
  the two profiles are of different devices: /device:TPU:5 before, /device:TPU:8 now
where the time goes in v3:
time: 64.8 us; the launch traced here: 64.7 us
  Pallas kernels  39.3 us (61%)
  waiting for transfers between devices  10.1 us (16%)
  starting transfers between devices  9.81 us (15%)
  other arithmetic  2.55 us (4%)
  local copies, waits for them, and re-layouts  1.6 us (2%)
  between operations  0.73 us (1%)
    pallas_call x1, Pallas kernels, translate(): pl.pallas_call(functools.partial(translate_kernel, variants, coarse_tile,...  34.1 us
    all_to_all x2, waiting for transfers between devices, exchange(): return lax.all_to_all(x, AXES, split_axis=0, concat_axis=0, tiled=True)  10.1 us
    all_to_all x2, starting transfers between devices, exchange(): return lax.all_to_all(x, AXES, split_axis=0, concat_axis=0, tiled=True)  9.81 us
    pallas_call x1, Pallas kernels, plan(): pl.pallas_call(functools.partial(plan_kernel, variants, coarse_at), out_s...  2.37 us
    unnamed x8, local copies, waits for them, and re-layouts  1.6 us
    pallas_call x1, Pallas kernels, join_asks(): pl.pallas_call(functools.partial(asks_kernel, fine_own), out_shape=shape_...  1.45 us
    pallas_call x1, Pallas kernels, answer(): pl.pallas_call(answer_kernel, in_specs=[whole(wanted), whole(fine_rows),...  1.36 us
  transfers between devices with their start and end apart: 2, of which 2 were waited for; matrix products, arithmetic and copies ran while one was open for 5% of the time, Pallas kernels for 4%

profile of v3, /device:TPU:8, one launch (start us, length us, event | category | flops | bytes accessed | tf_op | source)
XLA Modules:
  0.0 64.7 jit_solution(3262746348503433763)
XLA Ops:
  0.6 0.0 copy-start
  0.6 1.5 %join_asks.1 = s32[32,24]{1,0:T(8,128)} custom-call(s32[16,32]{1,0:T(8,128)} %bitcast.21, s32[8,32]{1,0:T(8,128)} %bitcast.23), custom_call_target="tpu_custom_call" | custom-call | tf_op jit(solution)/shard_map/join_asks/pallas_call | solution.py:48
  2.1 6.0 %all-to-all-start = ((s32[32,1,24]{2,1,0:T(1,128)}), s32[32,1,24]{2,1,0:T(1,128)S(1)}, u32[]{:S(2)}, u32[]{:S(2)}) async-start(s32[32,1,24]{2,1,0:T(1,128)} %bitcast.20), calls=%async_computation | async-start | bytes 32768 | tf_op jit(solution)/shard_map/all_to_all | solution.py:439
  8.2 0.8 %iota_compare_fusion = pred[144,8]{1,0:T(8,128)(4,1)S(1)} fusion(s32[144]{0:T(256)} %param.11), kind=kLoop, calls=%fused_computation.5 | loop fusion | flops 1152 | bytes 1728 | tf_op jit(solution)/shard_map/eq | solution.py:463
  8.9 0.7 %broadcast_subtract_fusion = s32[144]{0:T(256)S(1)} fusion(s32[144]{0:T(256)} %param.10, s32[]{:T(128)S(6)} %mul.7), kind=kLoop, calls=%fused_computation.8 | loop fusion | flops 144 | bytes 1156 | tf_op jit(solution)/shard_map/sub | solution.py:473
  9.6 1.1 %broadcast_select_fusion = bf16[144,8,152]{2,1,0:T(8,128)(2,1)S(1)} fusion(pred[144,8]{1,0:T(8,128)(4,1)S(1)} %iota_compare_fusion, bf16[144,152]{1,0:T(8,128)(2,1)} %bitcast.16), kind=kLoop, calls=%fused_computation.4 | loop fusion | flops 175104 | bytes 395136 | tf_op jit(solution)/shard_map/jit(_where)/select_n | solution.py:462
  10.7 0.0 copy-done
  10.7 0.4 convolution_bitcast_fusion
  11.2 0.2 convolution_convert_fusion.c_any.c_ref
  11.3 0.0 copy-start.2
  11.4 2.6 %all-to-all-done = s32[32,1,24]{2,1,0:T(1,128)S(1)} async-done(((s32[32,1,24]{2,1,0:T(1,128)}), s32[32,1,24]{2,1,0:T(1,128)S(1)}, u32[]{:S(2)}, u32[]{:S(2)}) %all-to-all-start) | async-done | bytes 3104 | tf_op jit(solution)/shard_map/all_to_all | solution.py:439
  14.0 0.0 copy-start.1
  14.0 0.9 %copy-done.1 = bf16[152,144]{0,1:T(8,128)(2,1)S(1)} copy-done((bf16[152,144]{0,1:T(8,128)(2,1)S(1)}, bf16[152,144]{0,1:T(8,128)(2,1)}, u32[]{:S(2)}) %copy-start.1) | copy-done | bytes 43800
  14.8 1.4 %answer.1 = bf16[32,32,128]{2,1,0:T(8,128)(2,1)} custom-call(s32[32,24]{1,0:T(8,128)S(1)} %bitcast.19, bf16[144,152]{1,0:T(8,128)(2,1)S(1)} %bitcast.18, bf16[32,152]{1,0:T(8,128)(2,1)S(1)} %convolution_convert_fusion.c_any.c_ref), custom_call_target="tpu_custom_call" | custom-call | tf_op jit(solution)/shard_map/answer/pallas_call | solution.py:89
  16.2 3.8 %all-to-all-start.1 = ((bf16[32,32,128]{2,1,0:T(8,128)(2,1)}), bf16[32,32,128]{2,1,0:T(8,128)(2,1)S(1)}, u32[]{:S(2)}, u32[]{:S(2)}) async-start(bf16[32,32,128]{2,1,0:T(8,128)(2,1)} %answer.1), calls=%async_computation.1 | async-start | bytes 524288 | tf_op jit(solution)/shard_map/all_to_all | solution.py:439
  20.0 2.4 %plan.1 = (s32[176,384]{1,0:T(8,128)}, s32[944,128]{1,0:T(8,128)}, s32[1]{0:T(128)}) custom-call(s32[16,32]{1,0:T(8,128)} %bitcast.22, s32[8,32]{1,0:T(8,128)} %bitcast.24, s32[144,316]{1,0:T(8,128)} %lf_ref.1, s32[32,316]{1,0:T(8,128)} %lc_ref.1), custom_call_target="tpu_custom_call" | custom-call | tf_op jit(solution)/shard_map/plan/pallas_call | solution.py:195
  22.4 7.5 %all-to-all-done.1.arrived_any = bf16[32,32,128]{2,1,0:T(8,128)(2,1)S(1)} async-done(((bf16[32,32,128]{2,1,0:T(8,128)(2,1)}), bf16[32,32,128]{2,1,0:T(8,128)(2,1)S(1)}, u32[]{:S(2)}, u32[]{:S(2)}) %all-to-all-start.1) | async-done | bytes 262176 | tf_op jit(solution)/shard_map/all_to_all | solution.py:439
  29.9 0.0 copy-start.3
  29.9 0.0 copy-done.2
  29.9 0.7 %copy-done.3 = bf16[32,32,128]{2,1,0:T(8,128)(2,1)} copy-done((bf16[32,32,128]{2,1,0:T(8,128)(2,1)}, bf16[32,32,128]{2,1,0:T(8,128)(2,1)S(1)}, u32[]{:S(2)}) %copy-start.3) | copy-done | bytes 262168
  30.6 34.1 %translate.1 = (f32[144,152]{1,0:T(8,128)}, f32[32,152]{1,0:T(8,128)}) custom-call(s32[1]{0:T(128)} %get-tuple-element.7.pick_ref, s32[176,384]{1,0:T(8,128)} %get-tuple-element.8.idx_ref, s32[944,128]{1,0:T(8,128)} %get-tuple-element.9.to_ref, bf16[144,152]{1,0:T(8,128)(2,1)} %bitcast.17, bf16[32,152]{1,0:T(8,128)(2,1)} %copy-done.2, ...), custom_call_target="tpu_custom_call" | custom-call | flops 3122921472 | bytes 17743872 | tf_op jit(solution)/shard_map/translate/pallas_call | solution.py:396
Async XLA Ops:
  0.6 10.1 %copy-start = (bf16[152,8,152]{2,1,0:T(8,128)(2,1)S(1)}, bf16[152,8,152]{2,1,0:T(8,128)(2,1)}, u32[]{:S(2)}) copy-start(bf16[152,8,152]{2,1,0:T(8,128)(2,1)} %param.12) | copy-start | bytes 1108996
  2.1 11.9 %all-to-all-start = ((s32[32,1,24]{2,1,0:T(1,128)}), s32[32,1,24]{2,1,0:T(1,128)S(1)}, u32[]{:S(2)}, u32[]{:S(2)}) async-start(s32[32,1,24]{2,1,0:T(1,128)} %bitcast.20), calls=%async_computation | async-start | bytes 32768 | tf_op jit(solution)/shard_map/all_to_all | solution.py:439
  11.3 18.5 %copy-start.2 = (bf16[32,152]{1,0:T(8,128)(2,1)}, bf16[32,152]{1,0:T(8,128)(2,1)S(1)}, u32[]{:S(2)}) copy-start(bf16[32,152]{1,0:T(8,128)(2,1)S(1)} %convolution_convert_fusion.c_any.c_ref) | copy-start | bytes 29188
  14.0 0.9 %copy-start.1 = (bf16[152,144]{0,1:T(8,128)(2,1)S(1)}, bf16[152,144]{0,1:T(8,128)(2,1)}, u32[]{:S(2)}) copy-start(bf16[152,144]{0,1:T(8,128)(2,1)} %param.9) | copy-start | bytes 131332
  16.2 13.7 %all-to-all-start.1 = ((bf16[32,32,128]{2,1,0:T(8,128)(2,1)}), bf16[32,32,128]{2,1,0:T(8,128)(2,1)S(1)}, u32[]{:S(2)}, u32[]{:S(2)}) async-start(bf16[32,32,128]{2,1,0:T(8,128)(2,1)} %answer.1), calls=%async_computation.1 | async-start | bytes 524288 | tf_op jit(solution)/shard_map/all_to_all | solution.py:439
  29.9 0.7 %copy-start.3 = (bf16[32,32,128]{2,1,0:T(8,128)(2,1)}, bf16[32,32,128]{2,1,0:T(8,128)(2,1)S(1)}, u32[]{:S(2)}) copy-start(bf16[32,32,128]{2,1,0:T(8,128)(2,1)S(1)} %all-to-all-done.1.arrived_any) | copy-start | bytes 786436
